TPU v7x, 32 devices: a whole 2x2x4 slice. The times are simulated.
32 devices in a mesh: copies: 2 (over y), row: 4 (over z), col: 4 (over x, core).
Axes of the slice: x: 2, y: 2, z: 4, core: 2. Of those that a mesh axis runs over, the one named last changes fastest.
Arguments:
- multiple_alignment_tensor: bfloat16 [128, 128, 256], P(('copies', 'col'), 'row'), parts along dimension 0, may hold values from -1000 to 1000
- standardize_multiplier: float32 [256], replicated, may hold values from 0.1 to 1.9
- standardize_shift: float32 [256], replicated, may hold values from -3 to 3
- lhs_embedding_matrix: bfloat16 [256, 32], replicated, may hold values from -0.375 to 0.375
- lhs_embedding_shift: float32 [32], replicated, may hold values from -4 to 4
- rhs_embedding_matrix: bfloat16 [256, 32], replicated, may hold values from -0.375 to 0.375
- rhs_embedding_shift: float32 [32], replicated, may hold values from -4 to 4
- final_mapping_matrix: bfloat16 [1024, 128], replicated, may hold values from -0.1875 to 0.1875
- final_mapping_shift: float32 [128], replicated, may hold values from -3 to 3
Outputs:
- pair_update: bfloat16 [256, 128, 128], P(('copies', 'row'), 'col'), parts along dimension 0
There are 2 independent parts, one for each index of `copies`. A program takes and returns all parts, laid end to end along the dimension named above; an argument that names none is the same for every part. Nothing has to cross between parts.
All inputs are finite; a program needn't handle non-finite values.
Results may differ from a plain program's by a relative error of at most 0.005.
Values may be sent and summed in bfloat16 or wider, within the bound.
A program may use at most 64 MiB of HBM per device.

v0:
```python
import math

import jax
import jax.numpy as jnp
from jax import lax
from jax.sharding import PartitionSpec as P


def from_root(value, axis, source):
    kept = jnp.where(lax.axis_index(axis) == source, value, 0).astype(value.dtype)
    return lax.psum(kept, axis)


def on_device(
    multiple_alignment_tensor,
    standardize_multiplier,
    standardize_shift,
    lhs_embedding_matrix,
    lhs_embedding_shift,
    rhs_embedding_matrix,
    rhs_embedding_shift,
    final_mapping_matrix,
    final_mapping_shift,
):
    homolog_shard, position_shard, feature_axes_group = multiple_alignment_tensor.shape
    hidden = lhs_embedding_matrix.shape[1]
    entries_collection = multiple_alignment_tensor.astype(jnp.float32)
    center = jnp.mean(entries_collection, axis=-1, keepdims=True)
    spread = jnp.mean((entries_collection - center) ** 2, axis=-1, keepdims=True)
    normed = (
        (entries_collection - center) * lax.rsqrt(spread + 1e-05) * standardize_multiplier
        + standardize_shift
    ).astype(jnp.bfloat16)
    left = (
        jnp.dot(normed, lhs_embedding_matrix, preferred_element_type=jnp.float32)
        + lhs_embedding_shift
    ).astype(jnp.bfloat16)
    right = (
        jnp.dot(normed, rhs_embedding_matrix, preferred_element_type=jnp.float32)
        + rhs_embedding_shift
    ).astype(jnp.bfloat16)
    left = left.reshape(homolog_shard, position_shard * hidden)
    right = right.reshape(homolog_shard, position_shard * hidden)
    ratio = lax.axis_size("row") // lax.axis_size("col")
    first_root = lax.axis_index("col") * ratio
    left_all, right_all = (
        lax.all_gather(left, "col", axis=0, tiled=True),
        lax.all_gather(right, "col", axis=0, tiled=True),
    )
    parts_list = []
    for offset in range(ratio):
        parts_list.append(from_root(right_all, "row", first_root + offset))
    right_cols = jnp.concatenate(parts_list, axis=1)
    seq_total = left_all.shape[0]
    col_res = right_cols.shape[1] // hidden
    step_cols = math.gcd(col_res, 32)
    width = step_cols * hidden
    count_blocks = col_res // step_cols
    pair_ch = final_mapping_matrix.shape[1]
    column_stack = right_cols.reshape(seq_total, count_blocks, width).transpose(1, 0, 2)

    def tile(block):
        outer = lax.dot_general(
            left_all, block, (((0,), (0,)), ((), ())), preferred_element_type=jnp.float32
        )
        outer = (outer / seq_total).astype(jnp.bfloat16)
        outer = outer.reshape(position_shard, hidden, step_cols, hidden).transpose(0, 2, 1, 3)
        outer = outer.reshape(position_shard * step_cols, hidden * hidden)
        pair = (
            jnp.dot(outer, final_mapping_matrix, preferred_element_type=jnp.float32)
            + final_mapping_shift
        )
        return pair.astype(jnp.bfloat16).reshape(position_shard, step_cols, pair_ch)

    tiles = lax.map(tile, column_stack)
    return tiles.transpose(1, 0, 2, 3).reshape(position_shard, col_res, pair_ch)


def solution(mesh):
    placed = (P(("copies", "col"), "row", None), P(), P(), P(), P(), P(), P(), P(), P())
    return jax.shard_map(
        on_device,
        mesh=mesh,
        in_specs=placed,
        out_specs=P(("copies", "row"), "col", None),
        check_vma=False,
    )
```

profile of v0, /device:TPU:0, one launch (start us, length us, event | category | flops | bytes accessed | tf_op | source)
XLA Modules:
  0.0 93.6 jit_solution(15924545689318369648)
XLA Ops:
  6.5 0.0 copy-start
  6.5 0.0 copy-start.1
  6.5 0.0 copy-start.3
  6.5 0.0 copy-start.4
  6.5 0.0 copy-start.5
  6.5 0.0 copy-start.2
  6.6 0.0 all-reduce.2.cloned.1.call-start
  6.6 1.1 %convert_reduce_fusion = f32[16,32]{1,0:T(8,128)S(1)} fusion(bf16[16,32,256]{2,1,0:T(8,128)(2,1)} %param.9), kind=kLoop, calls=%fused_computation.9 | loop fusion | flops 261632 | bytes 264192 | tf_op jit(solution)/shard_map/reduce_sum | solution.py:28
  7.8 1.2 %fusion.5 = f32[16,32]{1,0:T(8,128)S(1)} fusion(bf16[16,32,256]{2,1,0:T(8,128)(2,1)} %param.9, f32[16,32]{1,0:T(8,128)S(1)} %broadcast_multiply_fusion), kind=kLoop, calls=%fused_computation.12 | loop fusion | flops 523776 | bytes 266240 | tf_op jit(solution)/shard_map/reduce_sum | solution.py:29
  9.0 1.3 %fusion.2 = bf16[16,32,32]{2,1,0:T(8,128)(2,1)S(1)} fusion(f32[32]{0:T(128)} %param.15, bf16[16,32,256]{2,1,0:T(8,128)(2,1)} %param.9, f32[256]{0:T(256)} %param.11, f32[256]{0:T(256)} %param.10, f32[16,32]{1,0:T(8,128)S(1)} %add_rsqrt_fusion, f32[16,32]{1,0:T(8,128)S(1)} %broadcast_multiply_fusion, bf16[256,32]{0,1:T(8,128)(2,1)} %param.14), kind=kOutput, calls=%fused_computation.7 | convolution fusion | flops 9207808 | bytes 317568 | tf_op jit(solution)/shard_map/dot_general | solution.py:39
  10.3 0.2 reshape.38
  10.5 6.5 %all_gather.7 = bf16[64,1024]{1,0:T(8,128)(2,1)S(1)} all-gather(bf16[16,1024]{1,0:T(8,128)(2,1)S(1)} %reshape.38), channel_id=1, replica_groups=mesh['copies'=2,'row'=4,'col'=4] {'col'}, dimensions={0}, use_global_device_ids=true | all-gather | bytes 163840 | tf_op jit(solution)/shard_map/all_gather | solution.py:48
  17.0 0.7 broadcast_select_fusion
  17.6 0.0 all-reduce.2.cloned.1.call-update
  17.7 0.0 copy-done.1
  17.7 0.0 copy-done.3
  17.7 0.0 copy-done.4
  17.7 0.0 copy-done.5
  17.7 0.0 copy-done.2
  17.7 0.3 fusion.1
  18.0 0.2 reshape.37
  18.2 5.6 %all_gather.6 = bf16[64,1024]{1,0:T(8,128)(2,1)S(1)} all-gather(bf16[16,1024]{1,0:T(8,128)(2,1)S(1)} %reshape.37), channel_id=1, replica_groups=mesh['copies'=2,'row'=4,'col'=4] {'col'}, dimensions={0}, use_global_device_ids=true | all-gather | bytes 163840 | tf_op jit(solution)/shard_map/all_gather | solution.py:47
  23.8 30.1 %all-reduce.2.cloned.1.call-done = bf16[64,1024]{1,0:T(8,128)(2,1)} async-done(((bf16[64,1024]{1,0:T(8,128)(2,1)}), bf16[64,1024]{1,0:T(8,128)(2,1)}) %all-reduce.2.cloned.1.call-update) | async-done | bytes 131088 | tf_op jit(solution)/shard_map/psum | solution.py:11
  53.9 1.6 %multiply_convert_fusion = bf16[1024,1024]{1,0:T(8,128)(2,1)S(1)} fusion(bf16[64,1024]{1,0:T(8,128)(2,1)S(1)} %all_gather.6, bf16[64,1024]{1,0:T(8,128)(2,1)} %all-reduce.2.cloned.1.call-done), kind=kOutput, calls=%fused_computation.1 | convolution fusion | flops 136314880 | bytes 2359296 | tf_op jit(solution)/shard_map/while/body/eval_jaxpr/dot_general | solution.py:63
  55.5 7.9 %reshape.39 = bf16[32,32,32,32]{3,2,1,0:T(8,128)(2,1)} reshape(bf16[1024,1024]{1,0:T(8,128)(2,1)S(1)} %multiply_convert_fusion) | data formatting | bytes 4194304 | tf_op jit(solution)/shard_map/while/body/eval_jaxpr/reshape | solution.py:67
  63.5 10.5 %copy.12 = bf16[32,32,32,32]{3,1,2,0:T(8,128)(2,1)} copy(bf16[32,32,32,32]{3,2,1,0:T(8,128)(2,1)} %reshape.39) | data formatting | bytes 4194304 | tf_op jit(solution)/shard_map/while/body/eval_jaxpr/reshape | solution.py:67
  74.0 0.0 copy-start.6
  74.0 11.3 %reshape.40 = bf16[1024,1024]{1,0:T(8,128)(2,1)S(1)} reshape(bf16[32,32,32,32]{3,2,1,0:T(8,128)(2,1)} %bitcast.16) | data formatting | bytes 4194304 | tf_op jit(solution)/shard_map/while/body/eval_jaxpr/reshape | solution.py:68
  85.3 0.0 copy-done
  85.3 0.0 copy-done.6
  85.3 1.4 %fusion = bf16[1024,128]{1,0:T(8,128)(2,1)} fusion(bf16[1024,1024]{1,0:T(8,128)(2,1)S(1)} %reshape.40, bf16[1024,128]{1,0:T(8,128)(2,1)S(1)} %copy-done, f32[128]{0:T(128)S(1)} %copy-done.6), kind=kOutput, calls=%fused_computation.3 | convolution fusion | flops 268697600 | bytes 2621952 | tf_op jit(solution)/shard_map/while/body/eval_jaxpr/dot_general | solution.py:70
  (2 shorter events, 0.0 us)
Async XLA Ops:
  6.5 78.8 %copy-start = (bf16[1024,128]{1,0:T(8,128)(2,1)S(1)}, bf16[1024,128]{1,0:T(8,128)(2,1)}, u32[]{:S(2)}) copy-start(bf16[1024,128]{1,0:T(8,128)(2,1)} %param.16) | copy-start | bytes 786436
  6.5 11.1 %copy-start.1 = (bf16[16,32,256]{2,1,0:T(8,128)(2,1)S(1)}, bf16[16,32,256]{2,1,0:T(8,128)(2,1)}, u32[]{:S(2)}) copy-start(bf16[16,32,256]{2,1,0:T(8,128)(2,1)} %param.9) | copy-start | bytes 786436
  6.5 11.1 %copy-start.3 = (f32[256]{0:T(256)S(1)}, f32[256]{0:T(256)}, u32[]{:S(2)}) copy-start(f32[256]{0:T(256)} %param.11) | copy-start | bytes 3076
  6.5 11.1 %copy-start.4 = (f32[256]{0:T(256)S(1)}, f32[256]{0:T(256)}, u32[]{:S(2)}) copy-start(f32[256]{0:T(256)} %param.10) | copy-start | bytes 3076
  6.5 11.1 %copy-start.5 = (f32[32]{0:T(128)S(1)}, f32[32]{0:T(128)}, u32[]{:S(2)}) copy-start(f32[32]{0:T(128)} %param.13) | copy-start | bytes 388
  6.5 11.2 %copy-start.2 = (bf16[256,32]{0,1:T(8,128)(2,1)S(1)}, bf16[256,32]{0,1:T(8,128)(2,1)}, u32[]{:S(2)}) copy-start(bf16[256,32]{0,1:T(8,128)(2,1)} %param.12) | copy-start | bytes 49156
  6.6 47.4 %all-reduce.2.cloned.1.call-start = ((), (), s32[]{:S(2)}) async-start(), calls=%async_computation | async-start | bytes 262144 | tf_op jit(solution)/shard_map/psum | solution.py:11
  74.0 11.4 %copy-start.6 = (f32[128]{0:T(128)S(1)}, f32[128]{0:T(128)}, u32[]{:S(2)}) copy-start(f32[128]{0:T(128)} %param.17) | copy-start | bytes 1540
Sparse Core Ops, SparseCore 0:
  17.8 36.0 all-reduce.1
where the time goes:
time: 94 us; the launch traced here: 93.6 us
  local copies, waits for them, and re-layouts  30.1 us (32%)
  waiting for transfers between devices  30.1 us (32%)
  between operations  13.5 us (14%)
  blocking collectives  12.1 us (13%)
  matrix products  4.69 us (5%)
  other arithmetic  3.02 us (3%)
    psum x1, waiting for transfers between devices, from_root(): return lax.psum(kept, axis)  30.1 us
    reshape x2, local copies, waits for them, and re-layouts, tile(): outer.reshape(position_shard, hidden, step_cols, hidden)  18.4 us
    reshape x1, local copies, waits for them, and re-layouts, tile(): outer = outer.reshape(position_shard * step_cols, hidden * hidden)  11.3 us
    all_gather x1, blocking collectives, on_device(): lax.all_gather(right, 'col', axis=0, tiled=True)  6.48 us
    all_gather x1, blocking collectives, on_device(): lax.all_gather(left, 'col', axis=0, tiled=True)  5.6 us
  transfers between devices with their start and end apart: 1, of which 1 were waited for; matrix products, arithmetic and copies ran while one was open for 1% of the time, Pallas kernels for 0%

commit v1 on v0

v1 whole, which is shorter than its diff:
```python
import functools

import jax
import jax.numpy as jnp
from jax import lax
from jax.experimental import pallas as pl
from jax.experimental.pallas import tpu as pltpu
from jax.sharding import PartitionSpec as P

MESH = pl.DeviceIdType.MESH
LANES = 128
F32 = jnp.float32
BF16 = jnp.bfloat16


def each(count, body):
    if count <= 4:
        for index in range(count):
            body(index)
    else:
        lax.fori_loop(0, count, lambda index, carry: (body(index), carry)[1], 0)


def kernel(
    rows,
    cols,
    x_hbm,
    gain,
    bias,
    wl,
    bl,
    wr,
    br,
    w_hbm,
    bf,
    out,
    x_v,
    w_v,
    pl_v,
    pr_v,
    l_all,
    r_all,
    r_own,
    rt_v,
    wf_v,
    we_v,
    a_v,
    x_sem,
    w_sem,
    l_send,
    l_recv,
    r_send,
    r_recv,
):
    seqs, res, channels = x_v.shape
    hidden = wl.shape[1]
    groups = LANES // hidden
    tiles = res // groups
    ratio = rows // cols
    total = seqs * cols
    outs = bf.shape[1]
    copies_at = lax.axis_index("copies")
    row = lax.axis_index("row")
    col = lax.axis_index("col")
    target = row // ratio
    stays = col == target
    own = pl.ds(pl.multiple_of(col * seqs, seqs), seqs)

    x_copy = pltpu.make_async_copy(x_hbm, x_v, x_sem)
    x_copy.start()
    w_copy = pltpu.make_async_copy(w_hbm, w_v, w_sem)
    w_copy.start()

    barrier = pltpu.get_barrier_semaphore()

    def greet_left(step):
        peer = lax.rem(col + 1 + step, cols)
        pl.semaphore_signal(barrier, 1, device_id=(copies_at, row, peer), device_id_type=MESH)

    each(cols - 1, greet_left)

    def greet_right(step):
        source_row = col * ratio + step // cols
        source_col = lax.rem(step, cols)

        @pl.when(jnp.logical_not((source_row == row) & (source_col == col)))
        def _():
            pl.semaphore_signal(
                barrier, 1, device_id=(copies_at, source_row, source_col), device_id_type=MESH
            )

    each(ratio * cols, greet_right)

    w8 = jnp.concatenate([wl[...].astype(F32)] * groups + [wr[...].astype(F32)] * groups, axis=1).astype(BF16)
    bl4 = jnp.concatenate([bl[...]] * groups, axis=1)
    br4 = jnp.concatenate([br[...]] * groups, axis=1)
    block = lax.broadcasted_iota(jnp.int32, (seqs, LANES), 1) // hidden

    x_copy.wait()
    x = x_v[...].astype(F32).reshape(seqs * res, channels)
    center = jnp.mean(x, axis=-1, keepdims=True)
    moved = x - center
    spread = jnp.mean(moved * moved, axis=-1, keepdims=True)
    normed = (moved * lax.rsqrt(spread + 1e-05) * gain[...] + bias[...]).astype(BF16)
    projected = jnp.dot(normed, w8, preferred_element_type=F32)
    pl_v[...] = projected[:, :LANES]
    pr_v[...] = projected[:, LANES:]

    def spread_out(source, shift, tile):
        value = source[pl.ds(tile * groups, seqs, stride=res), :]
        for g in range(1, groups):
            value = jnp.where(block == g, source[pl.ds(tile * groups + g, seqs, stride=res), :], value)
        return (value + shift).astype(BF16)

    for tile in range(tiles):
        r_own[:, tile * LANES : (tile + 1) * LANES] = spread_out(pr_v, br4, tile)

    @pl.when(stays)
    def _():
        r_all[lax.rem(row, ratio), own, :] = r_own[...]

    pl.semaphore_wait(barrier, cols - 1 + rows - stays.astype(jnp.int32))

    def right_copy(step):
        return pltpu.make_async_remote_copy(
            src_ref=r_own,
            dst_ref=r_all.at[lax.rem(row, ratio), own],
            send_sem=r_send.at[step],
            recv_sem=r_recv.at[lax.rem(row, ratio), col],
            device_id=(copies_at, lax.rem(row + 1 + step, rows), target),
            device_id_type=MESH,
        )

    each(rows - 1, lambda step: right_copy(step).start())

    @pl.when(jnp.logical_not(stays))
    def _():
        right_copy(rows - 1).start()

    for tile in range(tiles):
        l_all[own, tile * LANES : (tile + 1) * LANES] = spread_out(pl_v, bl4, tile)

    def left_copy(step):
        return pltpu.make_async_remote_copy(
            src_ref=l_all.at[own],
            dst_ref=l_all.at[own],
            send_sem=l_send.at[step],
            recv_sem=l_recv.at[col],
            device_id=(copies_at, row, lax.rem(col + 1 + step, cols)),
            device_id_type=MESH,
        )

    each(cols - 1, lambda step: left_copy(step).start())

    w_copy.wait()
    wf_v[...] = w_v[...].astype(F32)
    for e in range(hidden):
        we_v[e * hidden : (e + 1) * hidden, :] = wf_v[pl.ds(e, hidden, stride=hidden), :].astype(BF16)

    def left_wait(step):
        peer = lax.rem(col + 1 + step, cols)
        rows_of = pl.ds(pl.multiple_of(peer * seqs, seqs), seqs)
        pltpu.make_async_remote_copy(
            src_ref=l_all.at[rows_of],
            dst_ref=l_all.at[rows_of],
            send_sem=l_send.at[step],
            recv_sem=l_recv.at[peer],
            device_id=(copies_at, row, peer),
            device_id_type=MESH,
        ).wait_recv()

    lane_block = lax.broadcasted_iota(jnp.int32, (hidden * res // groups, 2 * LANES), 1) // hidden
    low = lax.rem(lane_block, groups) < groups // 2
    even = lax.rem(lane_block, 2) == 0

    each(cols - 1, left_wait)

    def columns(index):
        def right_wait(peer):
            rows_of = pl.ds(peer * seqs, seqs)

            @pl.when(jnp.logical_not((col * ratio + index == row) & (col == peer)))
            def _():
                pltpu.make_async_remote_copy(
                    src_ref=r_own,
                    dst_ref=r_all.at[index, rows_of],
                    send_sem=r_send.at[0],
                    recv_sem=r_recv.at[index, peer],
                    device_id=(copies_at, row, col),
                    device_id_type=MESH,
                ).wait_recv()

        for peer in range(cols):
            right_wait(peer)
        for tile in range(tiles):
            piece = r_all[index, :, tile * LANES : (tile + 1) * LANES].astype(F32)
            rt_v[tile * LANES : (tile + 1) * LANES, :total] = piece.T
        lhs = []
        for low_e in range(groups):
            parts = [
                rt_v[pl.ds(high * groups + low_e, res, stride=hidden), :].astype(BF16)
                for high in range(hidden // groups)
            ]
            lhs.append(jnp.concatenate(parts, axis=0)[:, :total])
        for pair in range(tiles // 2):
            outer = []
            for low_e in range(groups):
                rhs = []
                for tile in (2 * pair, 2 * pair + 1):
                    piece = l_all[:, tile * LANES : (tile + 1) * LANES]
                    if low_e:
                        piece = pltpu.roll(piece.astype(F32), low_e * hidden, 1).astype(BF16)
                    rhs.append(piece)
                rhs = jnp.concatenate(rhs, axis=1)
                outer.append(jnp.dot(lhs[low_e], rhs, preferred_element_type=F32).astype(BF16))
            half = [jnp.where(low, outer[-k % 4], outer[(2 - k) % 4]) for k in range(groups)]
            for low_i in range(groups):
                mixed = jnp.where(even, half[low_i], half[low_i - 1])
                for t in range(2):
                    tile = 2 * pair + t
                    for high in range(hidden // groups):
                        a_v[low_i, tile * res : (tile + 1) * res, high * LANES : (high + 1) * LANES] = mixed[
                            high * res : (high + 1) * res, t * LANES : (t + 1) * LANES
                        ]
        for low_i in range(groups):
            weights = jnp.concatenate(
                [
                    we_v[e * hidden : (e + 1) * hidden, :]
                    for high in range(hidden // groups)
                    for e in [high * groups + (b - low_i) % groups for b in range(groups)]
                ],
                axis=0,
            )
            result = jnp.dot(a_v[low_i], weights, preferred_element_type=F32)
            result = (result * (1.0 / total) + bf[...]).astype(BF16)
            for tile in range(tiles):
                at = pl.ds(pl.multiple_of(index * res, res), res)
                out[tile * groups + low_i, at, :] = result[tile * res : (tile + 1) * res, :]

    each(ratio, columns)

    each(rows - 1, lambda step: right_copy(step).wait_send())

    @pl.when(jnp.logical_not(stays))
    def _():
        right_copy(rows - 1).wait_send()

    each(cols - 1, lambda step: left_copy(step).wait_send())


def solution(mesh):
    rows, cols = mesh.shape["row"], mesh.shape["col"]

    def on_device(x, gain, bias, wl, bl, wr, br, w, bf):
        seqs, res, channels = x.shape
        hidden = wl.shape[1]
        outs = w.shape[1]
        ratio = rows // cols
        total = seqs * cols
        wide = res * hidden
        vmem = pl.BlockSpec(memory_space=pltpu.VMEM)
        hbm = pl.BlockSpec(memory_space=pl.ANY)
        groups = LANES // hidden
        return pl.pallas_call(
            functools.partial(kernel, rows, cols),
            out_shape=jax.ShapeDtypeStruct((res, ratio * res, outs), BF16),
            in_specs=[hbm] + [vmem] * 6 + [hbm, vmem],
            out_specs=vmem,
            scratch_shapes=[
                pltpu.VMEM((seqs, res, channels), BF16),
                pltpu.VMEM(w.shape, BF16),
                pltpu.VMEM((seqs * res, LANES), F32),
                pltpu.VMEM((seqs * res, LANES), F32),
                pltpu.VMEM((total, wide), BF16),
                pltpu.VMEM((ratio, total, wide), BF16),
                pltpu.VMEM((seqs, wide), BF16),
                pltpu.VMEM((wide, LANES), F32),
                pltpu.VMEM(w.shape, F32),
                pltpu.VMEM(w.shape, BF16),
                pltpu.VMEM((groups, wide // groups, hidden * hidden), BF16),
                pltpu.SemaphoreType.DMA,
                pltpu.SemaphoreType.DMA,
                pltpu.SemaphoreType.DMA((cols - 1,)),
                pltpu.SemaphoreType.DMA((cols,)),
                pltpu.SemaphoreType.DMA((rows,)),
                pltpu.SemaphoreType.DMA((ratio, cols)),
            ],
            compiler_params=pltpu.CompilerParams(
                collective_id=0, has_side_effects=True, vmem_limit_bytes=48 * 1024 * 1024
            ),
        )(x, gain[None], bias[None], wl, bl[None], wr, br[None], w, bf[None])

    placed = (P(("copies", "col"), "row", None), P(), P(), P(), P(), P(), P(), P(), P())
    return jax.shard_map(
        on_device,
        mesh=mesh,
        in_specs=placed,
        out_specs=P(("copies", "row"), "col", None),
        check_vma=False,
    )
```

time: 94 us -> 16.2 us (0.17)
  waiting for transfers between devices: 30.1 us -> 0 us
  local copies, waits for them, and re-layouts: 30.1 us -> 4.13 us
  between operations: 13.5 us -> 0.06 us
  blocking collectives: 12.1 us -> 0 us
  Pallas kernels: 0 us -> 11.7 us
  matrix products: 4.69 us -> 0 us
  other arithmetic: 3.02 us -> 0 us
    psum x1 -> x0, waiting for transfers between devices: 30.1 us -> none  [from_root(): return lax.psum(kept, axis)]
    reshape x5 -> x0, local copies, waits for them, and re-layouts: 30.1 us -> none  [the longest x2 18.4 us: tile(): outer.reshape(position_shard, hidden, step_cols, hidden)]
    all_gather x2 -> x0, blocking collectives: 12.1 us -> none  [the longest x1 6.48 us: on_device(): lax.all_gather(right, 'col', axis=0, tiled=True)]
    pallas_call x0 -> x1, Pallas kernels: none -> 11.7 us  [on_device(): pl.pallas_call(functools.partial(kernel, rows, cols), out_shape=jax.Shape...]
    dot_general x4 -> x0, matrix products: 4.69 us -> none  [the longest x1 1.63 us: tile(): lax.dot_general(left_all, block, (((0,), (0,)), ((), ())), preferred_elem...]
    unnamed x14 -> x19, local copies, waits for them, and re-layouts: 0.03 us -> 4.13 us
    reduce_sum x2 -> x0, other arithmetic: 2.34 us -> none  [the longest x1 1.21 us: on_device(): jnp.mean((entries_collection - center) ** 2, axis=-1, keepdims=True)]
  transfers between devices with their start and end apart: 1 -> 0, of which waited for: 1 -> 0; matrix products, arithmetic and copies ran while one was open for 1% -> 0% of each run, Pallas kernels for 0% -> 0%
where the time goes in v1:
time: 16.2 us; the launch traced here: 15.9 us
  Pallas kernels  11.7 us (72%)
  local copies, waits for them, and re-layouts  4.13 us (25%)
    pallas_call x1, Pallas kernels, on_device(): pl.pallas_call(functools.partial(kernel, rows, cols), out_shape=jax.Shape...  11.7 us
    unnamed x19, local copies, waits for them, and re-layouts  4.13 us

profile of v1, /device:TPU:0, one launch (start us, length us, event | category | flops | bytes accessed | tf_op | source)
XLA Modules:
  0.0 15.9 jit_solution(2363310126484640666)
XLA Ops:
  0.0 0.0 copy-start.7
  0.0 0.8 %copy.10.wl = bf16[256,32]{1,0:T(8,128)(2,1)S(1)} copy(bf16[256,32]{0,1:T(8,128)(2,1)} %param.12) | data formatting | bytes 32768 | tf_op args[3]
  0.9 0.0 copy-done.7
  0.9 0.0 copy-start.2
  0.9 0.0 copy-start.3
  0.9 0.0 copy-start.4
  0.9 0.0 copy-start.5
  0.9 0.0 copy-start.6
  0.9 0.1 copy.11.wr
  1.0 0.5 %copy-done.2 = f32[256]{0:T(256)S(1)} copy-done((f32[256]{0:T(256)S(1)}, f32[256]{0:T(256)}, u32[]{:S(2)}) %copy-start.2) | copy-done | bytes 1048
  1.5 0.0 copy-done.3
  1.6 0.0 copy-done.4
  1.6 0.0 copy-done.5
  1.6 0.0 copy-done.6
  1.6 0.0 copy-start
  1.6 0.9 %copy-done = bf16[16,32,256]{2,1,0:T(8,128)(2,1)S(1)} copy-done((bf16[16,32,256]{2,1,0:T(8,128)(2,1)S(1)}, bf16[16,32,256]{2,1,0:T(8,128)(2,1)}, u32[]{:S(2)}) %copy-start) | copy-done | bytes 262168
  2.5 0.0 copy-start.1
  2.5 0.9 %copy-done.1 = bf16[1024,128]{1,0:T(8,128)(2,1)S(1)} copy-done((bf16[1024,128]{1,0:T(8,128)(2,1)S(1)}, bf16[1024,128]{1,0:T(8,128)(2,1)}, u32[]{:S(2)}) %copy-start.1) | copy-done | bytes 262168
  3.5 11.7 %shard_map.91 = bf16[32,32,128]{2,1,0:T(8,128)(2,1)S(1)} custom-call(bf16[16,32,256]{2,1,0:T(8,128)(2,1)S(1)} %copy-done, f32[1,256]{1,0:T(1,128)S(1)} %bitcast.5, f32[1,256]{1,0:T(1,128)S(1)} %bitcast.6, bf16[256,32]{1,0:T(8,128)(2,1)S(1)} %copy.10.wl, f32[1,32]{1,0:T(1,128)S(1)} %bitcast.7, bf16[256,32]{1,0:T(8,128)(2,1)S(1)} %copy.11.wr, ...), custom_call_target="tpu_custom_call" | custom-call | tf_op jit(solution)/shard_map/pallas_call | solution.py:264
  15.2 0.7 %copy.13 = bf16[32,32,128]{2,1,0:T(8,128)(2,1)} copy(bf16[32,32,128]{2,1,0:T(8,128)(2,1)S(1)} %shard_map.91) | data formatting | bytes 524288
Async XLA Ops:
  0.0 0.9 %copy-start.7 = (bf16[256,32]{0,1:T(8,128)(2,1)S(1)}, bf16[256,32]{0,1:T(8,128)(2,1)}, u32[]{:S(2)}) copy-start(bf16[256,32]{0,1:T(8,128)(2,1)} %param.14) | copy-start | bytes 49156
  0.9 0.7 %copy-start.2 = (f32[256]{0:T(256)S(1)}, f32[256]{0:T(256)}, u32[]{:S(2)}) copy-start(f32[256]{0:T(256)} %param.10) | copy-start | bytes 3076
  0.9 0.7 %copy-start.3 = (f32[256]{0:T(256)S(1)}, f32[256]{0:T(256)}, u32[]{:S(2)}) copy-start(f32[256]{0:T(256)} %param.11) | copy-start | bytes 3076
  0.9 0.7 %copy-start.4 = (f32[32]{0:T(128)S(1)}, f32[32]{0:T(128)}, u32[]{:S(2)}) copy-start(f32[32]{0:T(128)} %param.13) | copy-start | bytes 388
  0.9 0.7 %copy-start.5 = (f32[32]{0:T(128)S(1)}, f32[32]{0:T(128)}, u32[]{:S(2)}) copy-start(f32[32]{0:T(128)} %param.15) | copy-start | bytes 388
  0.9 0.7 %copy-start.6 = (f32[128]{0:T(128)S(1)}, f32[128]{0:T(128)}, u32[]{:S(2)}) copy-start(f32[128]{0:T(128)} %param.17) | copy-start | bytes 1540
  1.6 0.9 %copy-start = (bf16[16,32,256]{2,1,0:T(8,128)(2,1)S(1)}, bf16[16,32,256]{2,1,0:T(8,128)(2,1)}, u32[]{:S(2)}) copy-start(bf16[16,32,256]{2,1,0:T(8,128)(2,1)} %x_hbm.1) | copy-start | bytes 786436
  2.5 0.9 %copy-start.1 = (bf16[1024,128]{1,0:T(8,128)(2,1)S(1)}, bf16[1024,128]{1,0:T(8,128)(2,1)}, u32[]{:S(2)}) copy-start(bf16[1024,128]{1,0:T(8,128)(2,1)} %w_hbm.1) | copy-start | bytes 786436

commit v2 on v1

--- a/solution.py
+++ b/solution.py
@@ -25,17 +25,22 @@
     rows,
     cols,
     x_hbm,
+    gain_hbm,
+    bias_hbm,
+    wl_hbm,
+    bl_hbm,
+    wr_hbm,
+    br_hbm,
+    w_hbm,
+    bf_hbm,
+    out,
+    x_v,
     gain,
     bias,
-    wl,
-    bl,
-    wr,
-    br,
-    w_hbm,
+    wlr,
+    blr,
+    w_v,
     bf,
-    out,
-    x_v,
-    w_v,
     pl_v,
     pr_v,
     l_all,
@@ -45,20 +50,18 @@
     wf_v,
     we_v,
     a_v,
-    x_sem,
-    w_sem,
+    in_sem,
     l_send,
     l_recv,
     r_send,
     r_recv,
 ):
     seqs, res, channels = x_v.shape
-    hidden = wl.shape[1]
+    hidden = wlr.shape[0] // 2
     groups = LANES // hidden
     tiles = res // groups
     ratio = rows // cols
     total = seqs * cols
-    outs = bf.shape[1]
     copies_at = lax.axis_index("copies")
     row = lax.axis_index("row")
     col = lax.axis_index("col")
@@ -66,10 +69,24 @@
     stays = col == target
     own = pl.ds(pl.multiple_of(col * seqs, seqs), seqs)
 
-    x_copy = pltpu.make_async_copy(x_hbm, x_v, x_sem)
-    x_copy.start()
-    w_copy = pltpu.make_async_copy(w_hbm, w_v, w_sem)
-    w_copy.start()
+    loads = [
+        pltpu.make_async_copy(source, place, in_sem.at[index])
+        for index, (source, place) in enumerate(
+            [
+                (x_hbm, x_v),
+                (wl_hbm, wlr.at[0:hidden]),
+                (wr_hbm, wlr.at[hidden : 2 * hidden]),
+                (gain_hbm, gain),
+                (bias_hbm, bias),
+                (bl_hbm, blr.at[0:1]),
+                (br_hbm, blr.at[1:2]),
+                (w_hbm, w_v),
+                (bf_hbm, bf),
+            ]
+        )
+    ]
+    for load in loads:
+        load.start()
 
     barrier = pltpu.get_barrier_semaphore()
 
@@ -91,18 +108,21 @@
 
     each(ratio * cols, greet_right)
 
-    w8 = jnp.concatenate([wl[...].astype(F32)] * groups + [wr[...].astype(F32)] * groups, axis=1).astype(BF16)
-    bl4 = jnp.concatenate([bl[...]] * groups, axis=1)
-    br4 = jnp.concatenate([br[...]] * groups, axis=1)
     block = lax.broadcasted_iota(jnp.int32, (seqs, LANES), 1) // hidden
 
-    x_copy.wait()
+    for load in loads[1:7]:
+        load.wait()
+    left_w, right_w = wlr[:hidden, :], wlr[hidden:, :]
+    w8 = jnp.concatenate([left_w] * groups + [right_w] * groups, axis=0)
+    bl4 = jnp.concatenate([blr[0:1, :]] * groups, axis=1)
+    br4 = jnp.concatenate([blr[1:2, :]] * groups, axis=1)
+    loads[0].wait()
     x = x_v[...].astype(F32).reshape(seqs * res, channels)
     center = jnp.mean(x, axis=-1, keepdims=True)
     moved = x - center
     spread = jnp.mean(moved * moved, axis=-1, keepdims=True)
     normed = (moved * lax.rsqrt(spread + 1e-05) * gain[...] + bias[...]).astype(BF16)
-    projected = jnp.dot(normed, w8, preferred_element_type=F32)
+    projected = lax.dot_general(normed, w8, (((1,), (1,)), ((), ())), preferred_element_type=F32)
     pl_v[...] = projected[:, :LANES]
     pr_v[...] = projected[:, LANES:]
 
@@ -152,7 +172,8 @@
 
     each(cols - 1, lambda step: left_copy(step).start())
 
-    w_copy.wait()
+    loads[7].wait()
+    loads[8].wait()
     wf_v[...] = w_v[...].astype(F32)
     for e in range(hidden):
         we_v[e * hidden : (e + 1) * hidden, :] = wf_v[pl.ds(e, hidden, stride=hidden), :].astype(BF16)
@@ -259,16 +280,21 @@
         total = seqs * cols
         wide = res * hidden
         vmem = pl.BlockSpec(memory_space=pltpu.VMEM)
-        hbm = pl.BlockSpec(memory_space=pl.ANY)
+        hbm = pl.BlockSpec(memory_space=pltpu.HBM)
         groups = LANES // hidden
         return pl.pallas_call(
             functools.partial(kernel, rows, cols),
-            out_shape=jax.ShapeDtypeStruct((res, ratio * res, outs), BF16),
-            in_specs=[hbm] + [vmem] * 6 + [hbm, vmem],
+            out_shape=pltpu.VMEM((res, ratio * res, outs), BF16),
+            in_specs=[hbm] * 9,
             out_specs=vmem,
             scratch_shapes=[
                 pltpu.VMEM((seqs, res, channels), BF16),
+                pltpu.VMEM((1, channels), F32),
+                pltpu.VMEM((1, channels), F32),
+                pltpu.VMEM((2 * hidden, channels), BF16),
+                pltpu.VMEM((2, hidden), F32),
                 pltpu.VMEM(w.shape, BF16),
+                pltpu.VMEM((1, outs), F32),
                 pltpu.VMEM((seqs * res, LANES), F32),
                 pltpu.VMEM((seqs * res, LANES), F32),
                 pltpu.VMEM((total, wide), BF16),
@@ -278,8 +304,7 @@
                 pltpu.VMEM(w.shape, F32),
                 pltpu.VMEM(w.shape, BF16),
                 pltpu.VMEM((groups, wide // groups, hidden * hidden), BF16),
-                pltpu.SemaphoreType.DMA,
-                pltpu.SemaphoreType.DMA,
+                pltpu.SemaphoreType.DMA((9,)),
                 pltpu.SemaphoreType.DMA((cols - 1,)),
                 pltpu.SemaphoreType.DMA((cols,)),
                 pltpu.SemaphoreType.DMA((rows,)),
@@ -288,7 +313,7 @@
             compiler_params=pltpu.CompilerParams(
                 collective_id=0, has_side_effects=True, vmem_limit_bytes=48 * 1024 * 1024
             ),
-        )(x, gain[None], bias[None], wl, bl[None], wr, br[None], w, bf[None])
+        )(*[pltpu.with_memory_space_constraint(v, pltpu.HBM) for v in (x, gain[None], bias[None], wl.T, bl[None], wr.T, br[None], w, bf[None])])
 
     placed = (P(("copies", "col"), "row", None), P(), P(), P(), P(), P(), P(), P(), P())
     return jax.shard_map(

time: 16.2 us -> 12.5 us (0.77); the launches traced: 15.9 us -> 12.4 us
  local copies, waits for them, and re-layouts: 4.13 us -> 0.71 us
    unnamed x19 -> x1, local copies, waits for them, and re-layouts: 4.13 us -> 0.71 us
where the time goes in v2:
time: 12.5 us; the launch traced here: 12.4 us
  Pallas kernels  11.7 us (94%)
  local copies, waits for them, and re-layouts  0.71 us (6%)
    pallas_call x1, Pallas kernels, on_device(): pl.pallas_call(functools.partial(kernel, rows, cols), out_shape=pltpu.VME...  11.7 us
    unnamed x1, local copies, waits for them, and re-layouts  0.71 us

profile of v2, /device:TPU:0, one launch (start us, length us, event | category | flops | bytes accessed | tf_op | source)
XLA Modules:
  0.0 12.4 jit_solution(7822769688197513685)
XLA Ops:
  0.0 11.7 %shard_map.91 = bf16[32,32,128]{2,1,0:T(8,128)(2,1)S(1)} custom-call(bf16[16,32,256]{2,1,0:T(8,128)(2,1)} %x_hbm.1, f32[1,256]{1,0:T(1,128)} %bitcast.9, f32[1,256]{1,0:T(1,128)} %bitcast.10, bf16[32,256]{1,0:T(8,128)(2,1)} %bitcast.7, f32[1,32]{1,0:T(1,128)} %bitcast.11, bf16[32,256]{1,0:T(8,128)(2,1)} %bitcast.8, f32[1,32]{1,0:T(1,128)} %bitcast.12, ...), custom_call_target="tpu_custom_call" | custom-call | tf_op jit(solution)/shard_map/pallas_call | solution.py:285
  11.7 0.7 %copy.11 = bf16[32,32,128]{2,1,0:T(8,128)(2,1)} copy(bf16[32,32,128]{2,1,0:T(8,128)(2,1)S(1)} %shard_map.91) | data formatting | bytes 524288

commit v3 on v2

--- a/solution.py
+++ b/solution.py
@@ -9,6 +9,7 @@
 
 MESH = pl.DeviceIdType.MESH
 LANES = 128
+X_PARTS = 1
 F32 = jnp.float32
 BF16 = jnp.bfloat16
 
@@ -49,7 +50,9 @@
     rt_v,
     wf_v,
     we_v,
+    rolled_v,
     a_v,
+    x_sem,
     in_sem,
     l_send,
     l_recv,
@@ -69,11 +72,30 @@
     stays = col == target
     own = pl.ds(pl.multiple_of(col * seqs, seqs), seqs)
 
+    barrier = pltpu.get_barrier_semaphore()
+
+    def greet_left(step):
+        peer = lax.rem(col + 1 + step, cols)
+        pl.semaphore_signal(barrier, 1, device_id=(copies_at, row, peer), device_id_type=MESH)
+
+    each(cols - 1, greet_left)
+
+    def greet_right(step):
+        source_row = col * ratio + step // cols
+        source_col = lax.rem(step, cols)
+
+        @pl.when(jnp.logical_not((source_row == row) & (source_col == col)))
+        def _():
+            pl.semaphore_signal(
+                barrier, 1, device_id=(copies_at, source_row, source_col), device_id_type=MESH
+            )
+
+    each(ratio * cols, greet_right)
+
     loads = [
         pltpu.make_async_copy(source, place, in_sem.at[index])
         for index, (source, place) in enumerate(
             [
-                (x_hbm, x_v),
                 (wl_hbm, wlr.at[0:hidden]),
                 (wr_hbm, wlr.at[hidden : 2 * hidden]),
                 (gain_hbm, gain),
@@ -85,46 +107,40 @@
             ]
         )
     ]
-    for load in loads:
+    x_part = seqs // X_PARTS
+    x_loads = [
+        pltpu.make_async_copy(
+            x_hbm.at[part * x_part : (part + 1) * x_part],
+            x_v.at[part * x_part : (part + 1) * x_part],
+            x_sem.at[part],
+        )
+        for part in range(X_PARTS)
+    ]
+    for load in x_loads + loads[:6]:
         load.start()
 
-    barrier = pltpu.get_barrier_semaphore()
-
-    def greet_left(step):
-        peer = lax.rem(col + 1 + step, cols)
-        pl.semaphore_signal(barrier, 1, device_id=(copies_at, row, peer), device_id_type=MESH)
-
-    each(cols - 1, greet_left)
-
-    def greet_right(step):
-        source_row = col * ratio + step // cols
-        source_col = lax.rem(step, cols)
-
-        @pl.when(jnp.logical_not((source_row == row) & (source_col == col)))
-        def _():
-            pl.semaphore_signal(
-                barrier, 1, device_id=(copies_at, source_row, source_col), device_id_type=MESH
-            )
-
-    each(ratio * cols, greet_right)
-
     block = lax.broadcasted_iota(jnp.int32, (seqs, LANES), 1) // hidden
 
-    for load in loads[1:7]:
+    for load in loads[:6]:
         load.wait()
     left_w, right_w = wlr[:hidden, :], wlr[hidden:, :]
     w8 = jnp.concatenate([left_w] * groups + [right_w] * groups, axis=0)
     bl4 = jnp.concatenate([blr[0:1, :]] * groups, axis=1)
     br4 = jnp.concatenate([blr[1:2, :]] * groups, axis=1)
-    loads[0].wait()
-    x = x_v[...].astype(F32).reshape(seqs * res, channels)
-    center = jnp.mean(x, axis=-1, keepdims=True)
-    moved = x - center
-    spread = jnp.mean(moved * moved, axis=-1, keepdims=True)
-    normed = (moved * lax.rsqrt(spread + 1e-05) * gain[...] + bias[...]).astype(BF16)
-    projected = lax.dot_general(normed, w8, (((1,), (1,)), ((), ())), preferred_element_type=F32)
-    pl_v[...] = projected[:, :LANES]
-    pr_v[...] = projected[:, LANES:]
+    for part in range(X_PARTS):
+        x_loads[part].wait()
+        if part == X_PARTS - 1:
+            loads[6].start()
+            loads[7].start()
+        x = x_v[part * x_part : (part + 1) * x_part].astype(F32).reshape(x_part * res, channels)
+        center = jnp.mean(x, axis=-1, keepdims=True)
+        moved = x - center
+        spread = jnp.mean(moved * moved, axis=-1, keepdims=True)
+        normed = (moved * lax.rsqrt(spread + 1e-05) * gain[...] + bias[...]).astype(BF16)
+        projected = lax.dot_general(normed, w8, (((1,), (1,)), ((), ())), preferred_element_type=F32)
+        at = slice(part * x_part * res, (part + 1) * x_part * res)
+        pl_v[at, :] = projected[:, :LANES]
+        pr_v[at, :] = projected[:, LANES:]
 
     def spread_out(source, shift, tile):
         value = source[pl.ds(tile * groups, seqs, stride=res), :]
@@ -138,6 +154,9 @@
     @pl.when(stays)
     def _():
         r_all[lax.rem(row, ratio), own, :] = r_own[...]
+
+    for tile in range(tiles):
+        l_all[own, tile * LANES : (tile + 1) * LANES] = spread_out(pl_v, bl4, tile)
 
     pl.semaphore_wait(barrier, cols - 1 + rows - stays.astype(jnp.int32))
 
@@ -157,9 +176,6 @@
     def _():
         right_copy(rows - 1).start()
 
-    for tile in range(tiles):
-        l_all[own, tile * LANES : (tile + 1) * LANES] = spread_out(pl_v, bl4, tile)
-
     def left_copy(step):
         return pltpu.make_async_remote_copy(
             src_ref=l_all.at[own],
@@ -172,8 +188,8 @@
 
     each(cols - 1, lambda step: left_copy(step).start())
 
+    loads[6].wait()
     loads[7].wait()
-    loads[8].wait()
     wf_v[...] = w_v[...].astype(F32)
     for e in range(hidden):
         we_v[e * hidden : (e + 1) * hidden, :] = wf_v[pl.ds(e, hidden, stride=hidden), :].astype(BF16)
@@ -190,11 +206,15 @@
             device_id_type=MESH,
         ).wait_recv()
 
-    lane_block = lax.broadcasted_iota(jnp.int32, (hidden * res // groups, 2 * LANES), 1) // hidden
-    low = lax.rem(lane_block, groups) < groups // 2
-    even = lax.rem(lane_block, 2) == 0
+    lane_block = lax.rem(lax.broadcasted_iota(jnp.int32, (total, 2 * LANES), 1) // hidden, groups)
 
     each(cols - 1, left_wait)
+    for tile in range(tiles):
+        lanes = slice(tile * LANES, (tile + 1) * LANES)
+        piece = l_all[:, lanes]
+        rolled_v[0, :, lanes] = piece
+        for low_e in range(1, groups):
+            rolled_v[low_e, :, lanes] = pltpu.roll(piece.astype(F32), low_e * hidden, 1).astype(BF16)
 
     def columns(index):
         def right_wait(peer):
@@ -216,31 +236,35 @@
         for tile in range(tiles):
             piece = r_all[index, :, tile * LANES : (tile + 1) * LANES].astype(F32)
             rt_v[tile * LANES : (tile + 1) * LANES, :total] = piece.T
-        lhs = []
-        for low_e in range(groups):
-            parts = [
-                rt_v[pl.ds(high * groups + low_e, res, stride=hidden), :].astype(BF16)
-                for high in range(hidden // groups)
-            ]
-            lhs.append(jnp.concatenate(parts, axis=0)[:, :total])
-        for pair in range(tiles // 2):
-            outer = []
-            for low_e in range(groups):
-                rhs = []
-                for tile in (2 * pair, 2 * pair + 1):
-                    piece = l_all[:, tile * LANES : (tile + 1) * LANES]
-                    if low_e:
-                        piece = pltpu.roll(piece.astype(F32), low_e * hidden, 1).astype(BF16)
-                    rhs.append(piece)
-                rhs = jnp.concatenate(rhs, axis=1)
-                outer.append(jnp.dot(lhs[low_e], rhs, preferred_element_type=F32).astype(BF16))
-            half = [jnp.where(low, outer[-k % 4], outer[(2 - k) % 4]) for k in range(groups)]
-            for low_i in range(groups):
-                mixed = jnp.where(even, half[low_i], half[low_i - 1])
+        highs = hidden // groups
+        lhs = jnp.concatenate(
+            [
+                jnp.concatenate(
+                    [
+                        rt_v[pl.ds(high * groups + low_e, res, stride=hidden), :][:, :total]
+                        for low_e in range(groups)
+                    ],
+                    axis=1,
+                ).astype(BF16)
+                for high in range(highs)
+            ],
+            axis=0,
+        )
+        for low_i in range(groups):
+            for pair in range(tiles // 2):
+                lanes = slice(2 * pair * LANES, 2 * (pair + 1) * LANES)
+                rhs = jnp.concatenate(
+                    [
+                        jnp.where(lane_block == (low_e + low_i) % groups, rolled_v[low_e, :, lanes], 0)
+                        for low_e in range(groups)
+                    ],
+                    axis=0,
+                )
+                outer = jnp.dot(lhs, rhs, preferred_element_type=F32).astype(BF16)
                 for t in range(2):
                     tile = 2 * pair + t
-                    for high in range(hidden // groups):
-                        a_v[low_i, tile * res : (tile + 1) * res, high * LANES : (high + 1) * LANES] = mixed[
+                    for high in range(highs):
+                        a_v[low_i, tile * res : (tile + 1) * res, high * LANES : (high + 1) * LANES] = outer[
                             high * res : (high + 1) * res, t * LANES : (t + 1) * LANES
                         ]
         for low_i in range(groups):
@@ -303,8 +327,10 @@
                 pltpu.VMEM((wide, LANES), F32),
                 pltpu.VMEM(w.shape, F32),
                 pltpu.VMEM(w.shape, BF16),
+                pltpu.VMEM((groups, total, wide), BF16),
                 pltpu.VMEM((groups, wide // groups, hidden * hidden), BF16),
-                pltpu.SemaphoreType.DMA((9,)),
+                pltpu.SemaphoreType.DMA((X_PARTS,)),
+                pltpu.SemaphoreType.DMA((8,)),
                 pltpu.SemaphoreType.DMA((cols - 1,)),
                 pltpu.SemaphoreType.DMA((cols,)),
                 pltpu.SemaphoreType.DMA((rows,)),

time: 12.5 us -> 12.6 us (level); the launches traced: 12.4 us -> 12.3 us
  no operation moved by 1% of the time
where the time goes in v3:
time: 12.6 us; the launch traced here: 12.3 us
  Pallas kernels  11.6 us (92%)
  local copies, waits for them, and re-layouts  0.71 us (6%)
    pallas_call x1, Pallas kernels, on_device(): pl.pallas_call(functools.partial(kernel, rows, cols), out_shape=pltpu.VME...  11.6 us
    unnamed x1, local copies, waits for them, and re-layouts  0.71 us

profile of v3, /device:TPU:0, one launch (start us, length us, event | category | flops | bytes accessed | tf_op | source)
XLA Modules:
  0.0 12.3 jit_solution(2757405957859356616)
XLA Ops:
  0.0 11.6 %shard_map.91 = bf16[32,32,128]{2,1,0:T(8,128)(2,1)S(1)} custom-call(bf16[16,32,256]{2,1,0:T(8,128)(2,1)} %x_hbm.1, f32[1,256]{1,0:T(1,128)} %bitcast.9, f32[1,256]{1,0:T(1,128)} %bitcast.10, bf16[32,256]{1,0:T(8,128)(2,1)} %bitcast.7, f32[1,32]{1,0:T(1,128)} %bitcast.11, bf16[32,256]{1,0:T(8,128)(2,1)} %bitcast.8, f32[1,32]{1,0:T(1,128)} %bitcast.12, ...), custom_call_target="tpu_custom_call" | custom-call | tf_op jit(solution)/shard_map/pallas_call | solution.py:309
  11.6 0.7 %copy.11 = bf16[32,32,128]{2,1,0:T(8,128)(2,1)} copy(bf16[32,32,128]{2,1,0:T(8,128)(2,1)S(1)} %shard_map.91) | data formatting | bytes 524288

commit v4 on v3

--- a/solution.py
+++ b/solution.py
@@ -65,6 +65,8 @@
     tiles = res // groups
     ratio = rows // cols
     total = seqs * cols
+    part = res // 2
+    wide_half = res * hidden // 2
     copies_at = lax.axis_index("copies")
     row = lax.axis_index("row")
     col = lax.axis_index("col")
@@ -110,11 +112,11 @@
     x_part = seqs // X_PARTS
     x_loads = [
         pltpu.make_async_copy(
-            x_hbm.at[part * x_part : (part + 1) * x_part],
-            x_v.at[part * x_part : (part + 1) * x_part],
-            x_sem.at[part],
-        )
-        for part in range(X_PARTS)
+            x_hbm.at[piece_of * x_part : (piece_of + 1) * x_part],
+            x_v.at[piece_of * x_part : (piece_of + 1) * x_part],
+            x_sem.at[piece_of],
+        )
+        for piece_of in range(X_PARTS)
     ]
     for load in x_loads + loads[:6]:
         load.start()
@@ -127,18 +129,18 @@
     w8 = jnp.concatenate([left_w] * groups + [right_w] * groups, axis=0)
     bl4 = jnp.concatenate([blr[0:1, :]] * groups, axis=1)
     br4 = jnp.concatenate([blr[1:2, :]] * groups, axis=1)
-    for part in range(X_PARTS):
-        x_loads[part].wait()
-        if part == X_PARTS - 1:
+    for piece_of in range(X_PARTS):
+        x_loads[piece_of].wait()
+        if piece_of == X_PARTS - 1:
             loads[6].start()
             loads[7].start()
-        x = x_v[part * x_part : (part + 1) * x_part].astype(F32).reshape(x_part * res, channels)
+        x = x_v[piece_of * x_part : (piece_of + 1) * x_part].astype(F32).reshape(x_part * res, channels)
         center = jnp.mean(x, axis=-1, keepdims=True)
         moved = x - center
         spread = jnp.mean(moved * moved, axis=-1, keepdims=True)
         normed = (moved * lax.rsqrt(spread + 1e-05) * gain[...] + bias[...]).astype(BF16)
         projected = lax.dot_general(normed, w8, (((1,), (1,)), ((), ())), preferred_element_type=F32)
-        at = slice(part * x_part * res, (part + 1) * x_part * res)
+        at = slice(piece_of * x_part * res, (piece_of + 1) * x_part * res)
         pl_v[at, :] = projected[:, :LANES]
         pr_v[at, :] = projected[:, LANES:]
 
@@ -160,21 +162,23 @@
 
     pl.semaphore_wait(barrier, cols - 1 + rows - stays.astype(jnp.int32))
 
-    def right_copy(step):
+    def right_copy(step, half):
+        lanes = slice(half * wide_half, (half + 1) * wide_half)
         return pltpu.make_async_remote_copy(
-            src_ref=r_own,
-            dst_ref=r_all.at[lax.rem(row, ratio), own],
-            send_sem=r_send.at[step],
-            recv_sem=r_recv.at[lax.rem(row, ratio), col],
+            src_ref=r_own.at[:, lanes],
+            dst_ref=r_all.at[lax.rem(row, ratio), own, lanes],
+            send_sem=r_send.at[half, step],
+            recv_sem=r_recv.at[half, lax.rem(row, ratio), col],
             device_id=(copies_at, lax.rem(row + 1 + step, rows), target),
             device_id_type=MESH,
         )
 
-    each(rows - 1, lambda step: right_copy(step).start())
-
-    @pl.when(jnp.logical_not(stays))
-    def _():
-        right_copy(rows - 1).start()
+    for half in range(2):
+        each(rows - 1, lambda step: right_copy(step, half).start())
+
+        @pl.when(jnp.logical_not(stays))
+        def _():
+            right_copy(rows - 1, half).start()
 
     def left_copy(step):
         return pltpu.make_async_remote_copy(
@@ -216,24 +220,26 @@
         for low_e in range(1, groups):
             rolled_v[low_e, :, lanes] = pltpu.roll(piece.astype(F32), low_e * hidden, 1).astype(BF16)
 
-    def columns(index):
+    def columns(index, half):
+        lanes_half = slice(half * wide_half, (half + 1) * wide_half)
+
         def right_wait(peer):
             rows_of = pl.ds(peer * seqs, seqs)
 
             @pl.when(jnp.logical_not((col * ratio + index == row) & (col == peer)))
             def _():
                 pltpu.make_async_remote_copy(
-                    src_ref=r_own,
-                    dst_ref=r_all.at[index, rows_of],
-                    send_sem=r_send.at[0],
-                    recv_sem=r_recv.at[index, peer],
+                    src_ref=r_own.at[:, lanes_half],
+                    dst_ref=r_all.at[index, rows_of, lanes_half],
+                    send_sem=r_send.at[half, 0],
+                    recv_sem=r_recv.at[half, index, peer],
                     device_id=(copies_at, row, col),
                     device_id_type=MESH,
                 ).wait_recv()
 
         for peer in range(cols):
             right_wait(peer)
-        for tile in range(tiles):
+        for tile in range(half * tiles // 2, (half + 1) * tiles // 2):
             piece = r_all[index, :, tile * LANES : (tile + 1) * LANES].astype(F32)
             rt_v[tile * LANES : (tile + 1) * LANES, :total] = piece.T
         highs = hidden // groups
@@ -241,7 +247,7 @@
             [
                 jnp.concatenate(
                     [
-                        rt_v[pl.ds(high * groups + low_e, res, stride=hidden), :][:, :total]
+                        rt_v[pl.ds(half * wide_half + high * groups + low_e, part, stride=hidden), :][:, :total]
                         for low_e in range(groups)
                     ],
                     axis=1,
@@ -264,8 +270,8 @@
                 for t in range(2):
                     tile = 2 * pair + t
                     for high in range(highs):
-                        a_v[low_i, tile * res : (tile + 1) * res, high * LANES : (high + 1) * LANES] = outer[
-                            high * res : (high + 1) * res, t * LANES : (t + 1) * LANES
+                        a_v[low_i, tile * part : (tile + 1) * part, high * LANES : (high + 1) * LANES] = outer[
+                            high * part : (high + 1) * part, t * LANES : (t + 1) * LANES
                         ]
         for low_i in range(groups):
             weights = jnp.concatenate(
@@ -279,16 +285,18 @@
             result = jnp.dot(a_v[low_i], weights, preferred_element_type=F32)
             result = (result * (1.0 / total) + bf[...]).astype(BF16)
             for tile in range(tiles):
-                at = pl.ds(pl.multiple_of(index * res, res), res)
-                out[tile * groups + low_i, at, :] = result[tile * res : (tile + 1) * res, :]
-
-    each(ratio, columns)
-
-    each(rows - 1, lambda step: right_copy(step).wait_send())
-
-    @pl.when(jnp.logical_not(stays))
-    def _():
-        right_copy(rows - 1).wait_send()
+                at = pl.ds(pl.multiple_of(index * res + half * part, part), part)
+                out[tile * groups + low_i, at, :] = result[tile * part : (tile + 1) * part, :]
+
+    for half in range(2):
+        each(ratio, lambda index: columns(index, half))
+
+    for half in range(2):
+        each(rows - 1, lambda step: right_copy(step, half).wait_send())
+
+        @pl.when(jnp.logical_not(stays))
+        def _():
+            right_copy(rows - 1, half).wait_send()
 
     each(cols - 1, lambda step: left_copy(step).wait_send())
 
@@ -328,13 +336,13 @@
                 pltpu.VMEM(w.shape, F32),
                 pltpu.VMEM(w.shape, BF16),
                 pltpu.VMEM((groups, total, wide), BF16),
-                pltpu.VMEM((groups, wide // groups, hidden * hidden), BF16),
+                pltpu.VMEM((groups, wide // groups // 2, hidden * hidden), BF16),
                 pltpu.SemaphoreType.DMA((X_PARTS,)),
                 pltpu.SemaphoreType.DMA((8,)),
                 pltpu.SemaphoreType.DMA((cols - 1,)),
                 pltpu.SemaphoreType.DMA((cols,)),
-                pltpu.SemaphoreType.DMA((rows,)),
-                pltpu.SemaphoreType.DMA((ratio, cols)),
+                pltpu.SemaphoreType.DMA((2, rows)),
+                pltpu.SemaphoreType.DMA((2, ratio, cols)),
             ],
             compiler_params=pltpu.CompilerParams(
                 collective_id=0, has_side_effects=True, vmem_limit_bytes=48 * 1024 * 1024

time: 12.6 us -> 13 us (1.032)
  Pallas kernels: 11.6 us -> 12 us
    pallas_call x1, Pallas kernels: 11.6 us -> 12 us  [on_device(): pl.pallas_call(functools.partial(kernel, rows, cols), out_shape=pltpu.VME...]
where the time goes in v4:
time: 13 us; the launch traced here: 12.7 us
  Pallas kernels  12 us (92%)
  local copies, waits for them, and re-layouts  0.71 us (5%)
    pallas_call x1, Pallas kernels, on_device(): pl.pallas_call(functools.partial(kernel, rows, cols), out_shape=pltpu.VME...  12 us
    unnamed x1, local copies, waits for them, and re-layouts  0.71 us

profile of v4, /device:TPU:0, one launch (start us, length us, event | category | flops | bytes accessed | tf_op | source)
XLA Modules:
  0.0 12.7 jit_solution(10507665667853230040)
XLA Ops:
  0.0 12.0 %shard_map.91 = bf16[32,32,128]{2,1,0:T(8,128)(2,1)S(1)} custom-call(bf16[16,32,256]{2,1,0:T(8,128)(2,1)} %x_hbm.1, f32[1,256]{1,0:T(1,128)} %bitcast.9, f32[1,256]{1,0:T(1,128)} %bitcast.10, bf16[32,256]{1,0:T(8,128)(2,1)} %bitcast.7, f32[1,32]{1,0:T(1,128)} %bitcast.11, bf16[32,256]{1,0:T(8,128)(2,1)} %bitcast.8, f32[1,32]{1,0:T(1,128)} %bitcast.12, ...), custom_call_target="tpu_custom_call" | custom-call | tf_op jit(solution)/shard_map/pallas_call | solution.py:317
  12.0 0.7 %copy.11 = bf16[32,32,128]{2,1,0:T(8,128)(2,1)} copy(bf16[32,32,128]{2,1,0:T(8,128)(2,1)S(1)} %shard_map.91) | data formatting | bytes 524288
